TPU v7x, 32 devices: a whole 2x2x4 slice. The times are simulated.
32 devices in a mesh: groups: 2 (over y), cmp: 4 (over x, core), off: 4 (over z).
Axes of the slice: x: 2, y: 2, z: 4, core: 2. Of those that a mesh axis runs over, the one named last changes fastest.
Arguments:
- shot_traces: bfloat16 [8, 2048, 2048], P(('groups', 'off'), 'cmp'), parts along dimension 0, may hold values from -6 to 6
- trace_owner: int32 [8, 2048, 1], P(('groups', 'off'), 'cmp'), parts along dimension 0, may hold values from 0 to 3; in each aligned block of 512 rows (0 to 511, 512 to 1023, ..., all dimensions but the last counted through in order) at most 256 rows name the same one
- trace_bin: int32 [8, 2048], P(('groups', 'off'), 'cmp'), parts along dimension 0, may hold values from 0 to 127, as said below
- nmo_weight: bfloat16 [4, 16, 512, 128], P('off'), may hold values from -0.25 to 0.25
- band_start: int32 [4, 16], P('off'), may hold values from 0 to 1536, as said below
- mute_start: float32 [4], P('off'), may hold values from 0 to 1024
Outputs:
- stack: float32 [1024, 2048], P(('groups', 'cmp'), 'off'), parts along dimension 0
There are 2 independent parts, one for each index of `groups`. A program takes and returns all parts, laid end to end along the dimension named above; an argument that names none is the same for every part. Nothing has to cross between parts.
Inputs may be any that keep to these rules, and one draw needn't show every extreme that they name: `trace_owner`: among the 512 traces of one device, at most 256 have the same owner. `trace_bin`: some bins receive no trace at all. `band_start`: the band of window j starts at 128 * j plus less than 256, or at 1536 where that is earlier.
All inputs are finite; a program needn't handle non-finite values.
Results may differ from a plain program's by a relative error of at most 0.003.
Values may be sent and summed in bfloat16 or wider, within the bound.
A program may use at most 64 MiB of HBM per device.

v0:
```python
import jax
import jax.numpy as jnp
from jax import lax
from jax.sharding import PartitionSpec as P

BIN_DEV = 128


ramp_width = 64.0


def correct_traces(traces, weight, starts, mute_onset):
    pieces = []
    for window in range(weight.shape[0]):
        source = lax.dynamic_slice_in_dim(traces, starts[window], weight.shape[1], 1)
        pieces.append(jnp.dot(source, weight[window], preferred_element_type=jnp.float32))
    shifted = jnp.concatenate(pieces, axis=1)
    sample_time = jnp.arange(shifted.shape[1], dtype=jnp.float32)
    taper_curve = jnp.clip((sample_time - mute_onset) / ramp_width, 0.0, 1.0)
    return (shifted * taper_curve[None, :]).astype(jnp.bfloat16)


def stack_rows(flat_traces, flat_bins):
    selector = jnp.arange(BIN_DEV, dtype=jnp.int32)[:, None] == flat_bins[None, :]
    partial_stack = jnp.dot(
        selector.astype(jnp.bfloat16), flat_traces, preferred_element_type=jnp.float32
    )
    local_fold = jnp.sum(selector.astype(jnp.float32), axis=1)
    return (partial_stack, local_fold)


def on_device(shot_traces, trace_owner, trace_bin, nmo_weight, band_start, mute_start):
    peer_count = lax.axis_size("cmp")
    traces = shot_traces[0]
    owner_index = trace_owner[0, :, 0]
    local_bin = trace_bin[0]
    weight = nmo_weight[0]
    starts = band_start[0]
    mute_onset = mute_start[0]
    trace_count = traces.shape[0]
    samples = traces.shape[1]
    capacity = 2 * trace_count // peer_count
    member = (owner_index[:, None] == jnp.arange(peer_count, dtype=jnp.int32)[None, :]).astype(
        jnp.int32
    )
    earlier = jnp.cumsum(member, axis=0) - member
    slot_index = jnp.sum(earlier * member, axis=1)
    target = owner_index * capacity + slot_index
    bin_buffer = jnp.full((peer_count * capacity,), -1, jnp.int32).at[target].set(local_bin)
    bin_buffer = bin_buffer.reshape(peer_count, capacity)
    buffer = jnp.zeros((peer_count * capacity, samples), jnp.bfloat16).at[target].set(traces)
    slots = lax.all_to_all(
        buffer.reshape(peer_count, capacity, samples),
        "cmp",
        split_axis=0,
        concat_axis=0,
        tiled=True,
    )
    slot_bins = lax.all_to_all(bin_buffer, "cmp", split_axis=0, concat_axis=0, tiled=True)
    flat_slots = slots.reshape(-1, samples)
    repaired = correct_traces(flat_slots, weight, starts, mute_onset)
    arrived = repaired.reshape(slots.shape)
    partial_stack, local_fold = stack_rows(arrived.reshape(-1, samples), slot_bins.reshape(-1))
    fold_count = lax.psum(local_fold, "off")
    stack_share = lax.psum_scatter(partial_stack, "off", scatter_dimension=1, tiled=True)
    return stack_share / jnp.maximum(fold_count, 1.0)[:, None]


def solution(mesh):
    return jax.shard_map(
        on_device,
        mesh=mesh,
        in_specs=(
            P(("groups", "off"), "cmp", None),
            P(("groups", "off"), "cmp", None),
            P(("groups", "off"), "cmp"),
            P("off", None, None, None),
            P("off", None),
            P("off"),
        ),
        out_specs=P(("groups", "cmp"), "off"),
        check_vma=False,
    )
```

profile of v0, /device:TPU:0, one launch (start us, length us, event | category | flops | bytes accessed | tf_op | source)
XLA Modules:
  0.0 161.7 jit_solution(7785711588622265525)
XLA Ops:
  6.5 0.0 copy-start
  6.5 0.8 fusion.57
  7.4 1.2 reduce-window.6
  8.6 0.2 slice_reduce_fusion
  8.8 0.2 reduce-window.9
  9.0 0.1 add_bitcast_fusion
  9.1 0.7 fusion.56
  9.8 0.7 compare_select_fusion
  10.5 0.0 copy-done
  10.5 6.2 %scatter_custom_fusion.1 = bf16[1024,2048]{1,0:T(8,128)(2,1)} fusion(s32[512]{0:T(512)S(1)} %bitcast.108, bf16[1,512,2048]{2,1,0:T(8,128)(2,1)S(1)} %copy-done, bf16[]{:T(256)} %constant.5.clone.1), kind=kCustom, calls=%fused_computation.5 | custom fusion | bytes 6291458 | tf_op jit(solution)/shard_map/scatter | solution.py:51
  16.6 0.0 copy-start.2
  16.6 5.1 %all-to-all-start.1 = ((bf16[4,256,2048]{2,1,0:T(8,128)(2,1)}), bf16[4,256,2048]{2,1,0:T(8,128)(2,1)}, u32[]{:S(2)}, u32[]{:S(2)}) async-start(bf16[4,256,2048]{2,1,0:T(8,128)(2,1)} %bitcast.101), calls=%async_computation.1 | async-start | bytes 8388608 | tf_op jit(solution)/shard_map/all_to_all | solution.py:52
  21.7 0.0 copy-done.2
  21.7 0.7 fusion.76
  53.0 3.2 %scatter_custom_fusion = s32[1024]{0:T(1024)} fusion(s32[512]{0:T(512)S(1)} %bitcast.109, s32[512]{0:T(512)} %bitcast.110, s32[]{:T(128)} %constant.9.clone.1), kind=kCustom, calls=%fused_computation.104 | custom fusion | bytes 4608 | tf_op jit(solution)/shard_map/scatter | solution.py:49
  56.2 14.2 %all-to-all-done.1 = bf16[4,256,2048]{2,1,0:T(8,128)(2,1)} async-done(((bf16[4,256,2048]{2,1,0:T(8,128)(2,1)}), bf16[4,256,2048]{2,1,0:T(8,128)(2,1)}, u32[]{:S(2)}, u32[]{:S(2)}) %all-to-all-start.1) | async-done | bytes 4194336 | tf_op jit(solution)/shard_map/all_to_all | solution.py:52
  70.4 3.2 %all-to-all-start = ((s32[4,1,256]{2,1,0:T(1,128)}), s32[4,1,256]{2,1,0:T(1,128)S(1)}, u32[]{:S(2)}, u32[]{:S(2)}) async-start(s32[4,1,256]{2,1,0:T(1,128)} %bitcast.7), calls=%async_computation | async-start | bytes 8192 | tf_op jit(solution)/shard_map/all_to_all | solution.py:59
  73.7 0.2 reduce-scatter.2.cloned.1.call-start
  73.9 0.0 copy-start.1
  73.9 2.9 %convolution_dynamic-update-slice_fusion.15 = f32[1024,2048]{0,1:T(8,128)} fusion(bf16[1024,2048]{1,0:T(8,128)(2,1)} %bitcast.11, s32[]{:T(128)S(6)} %select_n.60, bf16[1,16,512,128]{3,2,1,0:T(8,128)(2,1)} %param.9), kind=kOutput, calls=%fused_computation.23 | convolution fusion | flops 134217728 | bytes 1703940 | tf_op jit(solution)/shard_map/dot_general | solution.py:16
  76.8 2.7 %convolution_dynamic-update-slice_fusion.14 = f32[1024,2048]{0,1:T(8,128)} fusion(f32[1024,2048]{0,1:T(8,128)} %convolution_dynamic-update-slice_fusion.15, bf16[1024,2048]{1,0:T(8,128)(2,1)} %bitcast.11, s32[]{:T(128)S(6)} %select_n.61, bf16[1,16,512,128]{3,2,1,0:T(8,128)(2,1)} %param.9), kind=kOutput, calls=%fused_computation.22 | convolution fusion | flops 134217728 | bytes 1703940 | tf_op jit(solution)/shard_map/dot_general | solution.py:16
  79.5 2.7 %convolution_dynamic-update-slice_fusion.13 = f32[1024,2048]{0,1:T(8,128)} fusion(f32[1024,2048]{0,1:T(8,128)} %convolution_dynamic-update-slice_fusion.14, bf16[1024,2048]{1,0:T(8,128)(2,1)} %bitcast.11, s32[]{:T(128)S(6)} %select_n.62, bf16[1,16,512,128]{3,2,1,0:T(8,128)(2,1)} %param.9), kind=kOutput, calls=%fused_computation.21 | convolution fusion | flops 134217728 | bytes 1703940 | tf_op jit(solution)/shard_map/dot_general | solution.py:16
  82.3 0.0 copy-done.1
  82.3 2.7 %convolution_dynamic-update-slice_fusion.12 = f32[1024,2048]{0,1:T(8,128)} fusion(f32[1024,2048]{0,1:T(8,128)} %convolution_dynamic-update-slice_fusion.13, bf16[1024,2048]{1,0:T(8,128)(2,1)} %bitcast.11, s32[]{:T(128)S(6)} %select_n.63, bf16[1,16,512,128]{3,2,1,0:T(8,128)(2,1)S(1)} %copy-done.1), kind=kOutput, calls=%fused_computation.20 | convolution fusion | flops 134217728 | bytes 1703940 | tf_op jit(solution)/shard_map/dot_general | solution.py:16
  85.0 2.7 %convolution_dynamic-update-slice_fusion.11 = f32[1024,2048]{0,1:T(8,128)} fusion(f32[1024,2048]{0,1:T(8,128)} %convolution_dynamic-update-slice_fusion.12, bf16[1024,2048]{1,0:T(8,128)(2,1)} %bitcast.11, s32[]{:T(128)S(6)} %select_n.64, bf16[1,16,512,128]{3,2,1,0:T(8,128)(2,1)S(1)} %copy-done.1), kind=kOutput, calls=%fused_computation.19 | convolution fusion | flops 134217728 | bytes 1703940 | tf_op jit(solution)/shard_map/dot_general | solution.py:16
  87.7 2.7 %convolution_dynamic-update-slice_fusion.10 = f32[1024,2048]{0,1:T(8,128)} fusion(f32[1024,2048]{0,1:T(8,128)} %convolution_dynamic-update-slice_fusion.11, bf16[1024,2048]{1,0:T(8,128)(2,1)} %bitcast.11, s32[]{:T(128)S(6)} %select_n.65, bf16[1,16,512,128]{3,2,1,0:T(8,128)(2,1)S(1)} %copy-done.1), kind=kOutput, calls=%fused_computation.18 | convolution fusion | flops 134217728 | bytes 1703940 | tf_op jit(solution)/shard_map/dot_general | solution.py:16
  90.4 2.7 %convolution_dynamic-update-slice_fusion.9 = f32[1024,2048]{0,1:T(8,128)} fusion(f32[1024,2048]{0,1:T(8,128)} %convolution_dynamic-update-slice_fusion.10, bf16[1024,2048]{1,0:T(8,128)(2,1)} %bitcast.11, s32[]{:T(128)S(6)} %select_n.66, bf16[1,16,512,128]{3,2,1,0:T(8,128)(2,1)S(1)} %copy-done.1), kind=kOutput, calls=%fused_computation.17 | convolution fusion | flops 134217728 | bytes 1703940 | tf_op jit(solution)/shard_map/dot_general | solution.py:16
  93.1 2.7 %convolution_dynamic-update-slice_fusion.8 = f32[1024,2048]{0,1:T(8,128)} fusion(f32[1024,2048]{0,1:T(8,128)} %convolution_dynamic-update-slice_fusion.9, bf16[1024,2048]{1,0:T(8,128)(2,1)} %bitcast.11, s32[]{:T(128)S(6)} %select_n.67, bf16[1,16,512,128]{3,2,1,0:T(8,128)(2,1)S(1)} %copy-done.1), kind=kOutput, calls=%fused_computation.16 | convolution fusion | flops 134217728 | bytes 1703940 | tf_op jit(solution)/shard_map/dot_general | solution.py:16
  95.9 2.7 %convolution_dynamic-update-slice_fusion.7 = f32[1024,2048]{0,1:T(8,128)} fusion(f32[1024,2048]{0,1:T(8,128)} %convolution_dynamic-update-slice_fusion.8, bf16[1024,2048]{1,0:T(8,128)(2,1)} %bitcast.11, s32[]{:T(128)S(6)} %select_n.68, bf16[1,16,512,128]{3,2,1,0:T(8,128)(2,1)S(1)} %copy-done.1), kind=kOutput, calls=%fused_computation.15 | convolution fusion | flops 134217728 | bytes 1703940 | tf_op jit(solution)/shard_map/dot_general | solution.py:16
  98.6 2.7 %convolution_dynamic-update-slice_fusion.6 = f32[1024,2048]{0,1:T(8,128)} fusion(f32[1024,2048]{0,1:T(8,128)} %convolution_dynamic-update-slice_fusion.7, bf16[1024,2048]{1,0:T(8,128)(2,1)} %bitcast.11, s32[]{:T(128)S(6)} %select_n.69, bf16[1,16,512,128]{3,2,1,0:T(8,128)(2,1)S(1)} %copy-done.1), kind=kOutput, calls=%fused_computation.14 | convolution fusion | flops 134217728 | bytes 1703940 | tf_op jit(solution)/shard_map/dot_general | solution.py:16
  101.3 2.7 %convolution_dynamic-update-slice_fusion.5 = f32[1024,2048]{0,1:T(8,128)} fusion(f32[1024,2048]{0,1:T(8,128)} %convolution_dynamic-update-slice_fusion.6, bf16[1024,2048]{1,0:T(8,128)(2,1)} %bitcast.11, s32[]{:T(128)S(6)} %select_n.70, bf16[1,16,512,128]{3,2,1,0:T(8,128)(2,1)S(1)} %copy-done.1), kind=kOutput, calls=%fused_computation.13 | convolution fusion | flops 134217728 | bytes 1703940 | tf_op jit(solution)/shard_map/dot_general | solution.py:16
  104.0 2.6 %convolution_dynamic-update-slice_fusion.4 = f32[1024,2048]{0,1:T(8,128)} fusion(f32[1024,2048]{0,1:T(8,128)} %convolution_dynamic-update-slice_fusion.5, bf16[1024,2048]{1,0:T(8,128)(2,1)} %bitcast.11, s32[]{:T(128)S(6)} %select_n.71, bf16[1,16,512,128]{3,2,1,0:T(8,128)(2,1)S(1)} %copy-done.1), kind=kOutput, calls=%fused_computation.12 | convolution fusion | flops 134217728 | bytes 1703940 | tf_op jit(solution)/shard_map/dot_general | solution.py:16
  106.6 2.6 %convolution_dynamic-update-slice_fusion.3 = f32[1024,2048]{0,1:T(8,128)} fusion(f32[1024,2048]{0,1:T(8,128)} %convolution_dynamic-update-slice_fusion.4, bf16[1024,2048]{1,0:T(8,128)(2,1)} %bitcast.11, s32[]{:T(128)S(6)} %select_n.72, bf16[1,16,512,128]{3,2,1,0:T(8,128)(2,1)S(1)} %copy-done.1), kind=kOutput, calls=%fused_computation.11 | convolution fusion | flops 134217728 | bytes 1703940 | tf_op jit(solution)/shard_map/dot_general | solution.py:16
  109.3 2.6 %convolution_dynamic-update-slice_fusion.2 = f32[1024,2048]{0,1:T(8,128)} fusion(f32[1024,2048]{0,1:T(8,128)} %convolution_dynamic-update-slice_fusion.3, bf16[1024,2048]{1,0:T(8,128)(2,1)} %bitcast.11, s32[]{:T(128)S(6)} %select_n.73, bf16[1,16,512,128]{3,2,1,0:T(8,128)(2,1)S(1)} %copy-done.1), kind=kOutput, calls=%fused_computation.10 | convolution fusion | flops 134217728 | bytes 1703940 | tf_op jit(solution)/shard_map/dot_general | solution.py:16
  111.9 2.6 %convolution_dynamic-update-slice_fusion.1 = f32[1024,2048]{0,1:T(8,128)} fusion(f32[1024,2048]{0,1:T(8,128)} %convolution_dynamic-update-slice_fusion.2, bf16[1024,2048]{1,0:T(8,128)(2,1)} %bitcast.11, s32[]{:T(128)S(6)} %select_n.74, bf16[1,16,512,128]{3,2,1,0:T(8,128)(2,1)S(1)} %copy-done.1), kind=kOutput, calls=%fused_computation.9 | convolution fusion | flops 134217728 | bytes 1703940 | tf_op jit(solution)/shard_map/dot_general | solution.py:16
  114.5 2.6 %convolution_dynamic-update-slice_fusion = f32[1024,2048]{0,1:T(8,128)} fusion(f32[1024,2048]{0,1:T(8,128)} %convolution_dynamic-update-slice_fusion.1, bf16[1024,2048]{1,0:T(8,128)(2,1)} %bitcast.11, s32[]{:T(128)S(6)} %select_n.75, bf16[1,16,512,128]{3,2,1,0:T(8,128)(2,1)S(1)} %copy-done.1), kind=kOutput, calls=%fused_computation.8 | convolution fusion | flops 134217728 | bytes 1703940 | tf_op jit(solution)/shard_map/dot_general | solution.py:16
  117.2 0.0 all-to-all-done
  117.2 6.0 %fusion = f32[128,2048]{1,0:T(8,128)} fusion(f32[1024,2048]{0,1:T(8,128)} %convolution_dynamic-update-slice_fusion, f32[2048]{0:T(1024)S(1)} %multiply_clamp_fusion, s32[1024]{0:T(1024)S(1)} %bitcast.102), kind=kOutput, calls=%fused_computation.3 | convolution fusion | flops 541196288 | bytes 9449472 | tf_op jit(solution)/shard_map/dot_general | solution.py:25
  123.2 0.0 reduce-scatter.2.cloned.1.call-update
  123.2 0.1 convert_reduce_fusion
  123.4 13.1 %psum.7 = f32[128]{0:T(128)S(1)} all-reduce(f32[128]{0:T(128)S(1)} %convert_reduce_fusion), channel_id=1, replica_groups=mesh['groups'=2,'cmp'=4,'off'=4] {'off'}, use_global_device_ids=true, to_apply=%region_7.8 | all-reduce | flops 128 | bytes 1024 | tf_op jit(solution)/shard_map/psum | solution.py:64
  136.5 16.6 %reduce-scatter.2.cloned.1.call-done = f32[128,512]{1,0:T(8,128)} async-done(((f32[128,2048]{1,0:T(8,128)}), f32[128,512]{1,0:T(8,128)}) %reduce-scatter.2.cloned.1.call-update) | async-done | bytes 262160 | tf_op jit(solution)/shard_map/reduce_scatter | solution.py:65
  153.1 1.7 %broadcast_divide_fusion = f32[128,512]{1,0:T(8,128)} fusion(f32[128,512]{1,0:T(8,128)} %reduce-scatter.2.cloned.1.call-done, f32[128]{0:T(128)S(1)} %broadcast_maximum_fusion), kind=kLoop, calls=%fused_computation.59 | loop fusion | flops 65536 | bytes 524800 | tf_op jit(solution)/shard_map/div | solution.py:66
  (2 shorter events, 0.0 us)
Async XLA Ops:
  6.5 3.9 %copy-start = (bf16[1,512,2048]{2,1,0:T(8,128)(2,1)S(1)}, bf16[1,512,2048]{2,1,0:T(8,128)(2,1)}, u32[]{:S(2)}) copy-start(bf16[1,512,2048]{2,1,0:T(8,128)(2,1)} %param.6) | copy-start | bytes 6291460
  16.6 5.1 %copy-start.2 = (s32[1,16]{1,0:T(1,128)S(1)}, s32[1,16]{1,0:T(1,128)}, u32[]{:S(2)}) copy-start(s32[1,16]{1,0:T(1,128)} %param.10) | copy-start | bytes 196
  16.6 53.8 %all-to-all-start.1 = ((bf16[4,256,2048]{2,1,0:T(8,128)(2,1)}), bf16[4,256,2048]{2,1,0:T(8,128)(2,1)}, u32[]{:S(2)}, u32[]{:S(2)}) async-start(bf16[4,256,2048]{2,1,0:T(8,128)(2,1)} %bitcast.101), calls=%async_computation.1 | async-start | bytes 8388608 | tf_op jit(solution)/shard_map/all_to_all | solution.py:52
  70.4 46.7 %all-to-all-start = ((s32[4,1,256]{2,1,0:T(1,128)}), s32[4,1,256]{2,1,0:T(1,128)S(1)}, u32[]{:S(2)}, u32[]{:S(2)}) async-start(s32[4,1,256]{2,1,0:T(1,128)} %bitcast.7), calls=%async_computation | async-start | bytes 8192 | tf_op jit(solution)/shard_map/all_to_all | solution.py:59
  73.7 79.4 %reduce-scatter.2.cloned.1.call-start = ((), (), s32[]{:S(2)}) async-start(), calls=%async_computation.3 | async-start | bytes 1310720 | tf_op jit(solution)/shard_map/reduce_scatter | solution.py:65
  73.9 8.3 %copy-start.1 = (bf16[1,16,512,128]{3,2,1,0:T(8,128)(2,1)S(1)}, bf16[1,16,512,128]{3,2,1,0:T(8,128)(2,1)}, u32[]{:S(2)}) copy-start(bf16[1,16,512,128]{3,2,1,0:T(8,128)(2,1)} %param.9) | copy-start | bytes 6291460
Sparse Core Ops, SparseCore 0:
  123.3 29.7 reduce-scatter.1
where the time goes:
time: 163 us; the launch traced here: 162 us
  matrix products  49.3 us (30%)
  between operations  44 us (27%)
  waiting for transfers between devices  30.9 us (19%)
  blocking collectives  13.1 us (8%)
  local copies, waits for them, and re-layouts  10.3 us (6%)
  starting transfers between devices  8.54 us (5%)
  other arithmetic  5.59 us (3%)
    dot_general x16, matrix products, correct_traces(): jnp.dot(source, weight[window], preferred_element_type=jnp.float32)  43.2 us
    reduce_scatter x1, waiting for transfers between devices, on_device(): lax.psum_scatter(partial_stack, 'off', scatter_dimension=1, tiled=True)  16.6 us
    all_to_all x1, waiting for transfers between devices, on_device(): lax.all_to_all(buffer.reshape(peer_count, capacity, samples), 'cmp', spli...  14.2 us
    psum x1, blocking collectives, on_device(): fold_count = lax.psum(local_fold, 'off')  13.1 us
    scatter x1, local copies, waits for them, and re-layouts, on_device(): jnp.zeros((peer_count * capacity, samples), jnp.bfloat16).at[target]  6.17 us
    dot_general x1, matrix products, stack_rows(): jnp.dot(selector.astype(jnp.bfloat16), flat_traces, preferred_element_typ...  6.03 us
    all_to_all x1, starting transfers between devices, on_device(): lax.all_to_all(buffer.reshape(peer_count, capacity, samples), 'cmp', spli...  5.07 us
  transfers between devices with their start and end apart: 3, of which 2 were waited for; matrix products, arithmetic and copies ran while one was open for 29% of the time, Pallas kernels for 0%

commit v1 on v0

--- a/solution.py
+++ b/solution.py
@@ -1,10 +1,14 @@
 import jax
 import jax.numpy as jnp
 from jax import lax
+from jax.experimental import pallas as pl
+from jax.experimental.pallas import tpu as pltpu
 from jax.sharding import PartitionSpec as P
 
+MESH = pl.DeviceIdType.MESH
 BIN_DEV = 128
-
+WIDTH = 256
+SPREAD = 384
 
 ramp_width = 64.0
 
@@ -66,9 +70,268 @@
     return stack_share / jnp.maximum(fold_count, 1.0)[:, None]
 
 
+def fused(
+    traces_hbm, weight_hbm, owner_ref, bin_ref, starts_ref, mute_ref,
+    out_ref, fold_ref,
+    traces, weight, padded, shifted_weight, selector,
+    keep_core, send_core, recv_core,
+    keep_x, send_x, recv_x, send_z, recv_z,
+    fold_core_out, fold_core_in, fold_x_out, fold_x_in, fold_z_in,
+    load_sem, weight_sem,
+    core_send_sem, core_recv_sem, x_send_sem, x_recv_sem, z_send_sem, z_recv_sem,
+    fold_send_sem, fold_recv_sem,
+):
+    rows, samples = traces.shape
+    span = weight.shape[2]
+    chunks = weight.shape[0]
+    c = lax.axis_index("cmp")
+    z = lax.axis_index("off")
+    nz = 4
+    core_peer = c + 1 - 2 * lax.rem(c, 2)
+    x_peer = lax.rem(c + 2, 4)
+    band = span + SPREAD
+
+    barrier = pltpu.get_barrier_semaphore()
+    pl.semaphore_signal(barrier, inc=1, device_id={"cmp": core_peer}, device_id_type=MESH)
+    pl.semaphore_signal(barrier, inc=1, device_id={"cmp": x_peer}, device_id_type=MESH)
+    for step in range(1, nz):
+        pl.semaphore_signal(
+            barrier, inc=1, device_id={"off": lax.rem(z + step, nz)}, device_id_type=MESH
+        )
+
+    def pair_of(m):
+        return 2 * lax.rem(z + 1 + m // 2, nz) + m % 2
+
+    load = pltpu.make_async_copy(traces_hbm, traces, load_sem)
+    load.start()
+
+    def weight_load(m):
+        return pltpu.make_async_copy(
+            weight_hbm.at[pl.ds(2 * pair_of(m), 2)], weight.at[m], weight_sem.at[m]
+        )
+
+    def begin(m, carry):
+        weight_load(m).start()
+        return carry
+
+    lax.fori_loop(0, chunks, begin, 0)
+
+    owner = owner_ref[...]
+    other_core = jnp.where(lax.rem(owner, 2) == lax.rem(c, 2), 0, 1)
+    other_x = jnp.where(owner // 2 == c // 2, 0, 1)
+    place = (2 * other_core + other_x) * BIN_DEV + bin_ref[...]
+    line = lax.broadcasted_iota(jnp.int32, (4 * BIN_DEV, rows), 0)
+    selector[...] = jnp.where(line == place, 1.0, 0.0).astype(jnp.bfloat16)
+    fold = lax.dot_general(
+        jnp.ones((8, rows), jnp.bfloat16),
+        selector[...],
+        (((1,), (1,)), ((), ())),
+        preferred_element_type=jnp.float32,
+    )
+    fold_core_out[...] = fold[:, 2 * BIN_DEV :]
+    padded[:, 0:SPREAD] = jnp.zeros((2, SPREAD, 128), jnp.float32)
+    padded[:, SPREAD + span :] = jnp.zeros((2, SPREAD, 128), jnp.float32)
+    load.wait()
+
+    def core_copy(m):
+        return pltpu.make_async_remote_copy(
+            src_ref=send_core.at[m], dst_ref=recv_core.at[m],
+            send_sem=core_send_sem.at[m], recv_sem=core_recv_sem.at[m],
+            device_id={"cmp": core_peer}, device_id_type=MESH,
+        )
+
+    def x_copy(m):
+        return pltpu.make_async_remote_copy(
+            src_ref=send_x.at[m], dst_ref=recv_x.at[m],
+            send_sem=x_send_sem.at[m], recv_sem=x_recv_sem.at[m],
+            device_id={"cmp": x_peer}, device_id_type=MESH,
+        )
+
+    def z_copy(m):
+        return pltpu.make_async_remote_copy(
+            src_ref=send_z.at[m], dst_ref=recv_z.at[m],
+            send_sem=z_send_sem.at[m], recv_sem=z_recv_sem.at[m],
+            device_id={"off": lax.rem(z + 1 + m // 2, nz)}, device_id_type=MESH,
+        )
+
+    def fold_copy(source, target, slot, device):
+        return pltpu.make_async_remote_copy(
+            src_ref=source, dst_ref=target,
+            send_sem=fold_send_sem.at[slot], recv_sem=fold_recv_sem.at[slot],
+            device_id=device, device_id_type=MESH,
+        )
+
+    def correct(m):
+        weight_load(m).wait()
+        first = pair_of(m) * WIDTH
+        base = jnp.minimum(first, samples - band)
+        for half in range(2):
+            start = starts_ref[2 * pair_of(m) + half]
+            lead = jnp.clip(start - base, 0, SPREAD)
+            padded[half, SPREAD : SPREAD + span] = weight[m, half].astype(jnp.float32)
+            shifted_weight[:, half * 128 : half * 128 + 128] = padded[
+                half, pl.ds(SPREAD - lead, band)
+            ].astype(jnp.bfloat16)
+        source = traces[:, pl.ds(pl.multiple_of(base, 128), band)]
+        shifted = jnp.dot(source, shifted_weight[...], preferred_element_type=jnp.float32)
+        time = first + lax.broadcasted_iota(jnp.int32, (1, WIDTH), 1)
+        taper = jnp.clip((time.astype(jnp.float32) - mute_ref[0]) / ramp_width, 0.0, 1.0)
+        corrected = (shifted * taper).astype(jnp.bfloat16)
+        partial = jnp.dot(selector[...], corrected, preferred_element_type=jnp.float32)
+        keep_core[m] = partial[: 2 * BIN_DEV]
+        send_core[m] = partial[2 * BIN_DEV :].astype(jnp.bfloat16)
+
+    def end_core(m):
+        core_copy(m).wait_recv()
+        total = keep_core[m] + recv_core[m].astype(jnp.float32)
+        keep_x[m] = total[:BIN_DEV]
+        send_x[m] = total[BIN_DEV:].astype(jnp.bfloat16)
+        x_copy(m).start()
+
+    def x_total(m):
+        x_copy(m).wait_recv()
+        return keep_x[m] + recv_x[m].astype(jnp.float32)
+
+    def end_x(m):
+        send_z[m] = x_total(m).astype(jnp.bfloat16)
+        z_copy(m).start()
+
+    correct(0)
+    pl.semaphore_wait(barrier, nz + 1)
+    core_copy(0).start()
+    fold_core = fold_copy(fold_core_out, fold_core_in, 0, {"cmp": core_peer})
+    fold_core.start()
+
+    def step(m, carry):
+        correct(m)
+        core_copy(m).start()
+        end_core(m - 1)
+
+        @pl.when(m >= 3)
+        def _():
+            end_x(m - 3)
+
+        return carry
+
+    lax.fori_loop(1, chunks, step, 0)
+    end_core(chunks - 1)
+
+    fold_core.wait_recv()
+    fold = fold[:, : 2 * BIN_DEV] + fold_core_in[...]
+    fold_x_out[0] = fold[:, BIN_DEV:]
+    fold_x = fold_copy(fold_x_out.at[0], fold_x_in, 1, {"cmp": x_peer})
+    fold_x.start()
+    for m in range(chunks - 3, chunks - 2):
+        end_x(m)
+    fold_x.wait_recv()
+    fold = fold[:, :BIN_DEV] + fold_x_in[...]
+    fold_x_out[1] = fold
+    fold_z = []
+    for away in range(1, nz):
+        copy = fold_copy(
+            fold_x_out.at[1], fold_z_in.at[away - 1], 1 + away, {"off": lax.rem(z + away, nz)}
+        )
+        copy.start()
+        fold_z.append(copy)
+
+    for half in range(2):
+        out_ref[:, half * WIDTH : half * WIDTH + WIDTH] = x_total(chunks - 2 + half)
+    for copy in fold_z:
+        copy.wait_recv()
+    for away in range(1, nz):
+        fold = fold + fold_z_in[away - 1]
+    fold_ref[...] = fold
+    for m in range(chunks - 2):
+        z_copy(m).wait_recv()
+        half = m % 2
+        out_ref[:, half * WIDTH : half * WIDTH + WIDTH] += recv_z[m].astype(jnp.float32)
+
+    def drain(m, carry):
+        core_copy(m).wait_send()
+        x_copy(m).wait_send()
+        return carry
+
+    lax.fori_loop(0, chunks, drain, 0)
+
+    def drain_z(m, carry):
+        z_copy(m).wait_send()
+        return carry
+
+    lax.fori_loop(0, chunks - 2, drain_z, 0)
+    fold_core.wait_send()
+    fold_x.wait_send()
+    for copy in fold_z:
+        copy.wait_send()
+
+
+def on_device_fused(shot_traces, trace_owner, trace_bin, nmo_weight, band_start, mute_start):
+    rows, samples = shot_traces.shape[1:]
+    windows, span, ws = nmo_weight.shape[1:]
+    chunks = samples // WIDTH
+    f32, bf16 = jnp.float32, jnp.bfloat16
+    any_space = pl.BlockSpec(memory_space=pl.ANY)
+    vmem = pl.BlockSpec(memory_space=pltpu.VMEM)
+    smem = pl.BlockSpec(memory_space=pltpu.SMEM)
+    dma = pltpu.SemaphoreType.DMA
+    totals, fold = pl.pallas_call(
+        fused,
+        out_shape=(
+            jax.ShapeDtypeStruct((BIN_DEV, samples // 4), f32),
+            jax.ShapeDtypeStruct((8, BIN_DEV), f32),
+        ),
+        in_specs=[any_space, any_space, vmem, vmem, smem, smem],
+        out_specs=(vmem, vmem),
+        scratch_shapes=[
+            pltpu.VMEM((rows, samples), bf16),
+            pltpu.VMEM((chunks, 2, span, ws), bf16),
+            pltpu.VMEM((2, span + 2 * SPREAD, ws), f32),
+            pltpu.VMEM((span + SPREAD, WIDTH), bf16),
+            pltpu.VMEM((4 * BIN_DEV, rows), bf16),
+            pltpu.VMEM((chunks, 2 * BIN_DEV, WIDTH), f32),
+            pltpu.VMEM((chunks, 2 * BIN_DEV, WIDTH), bf16),
+            pltpu.VMEM((chunks, 2 * BIN_DEV, WIDTH), bf16),
+            pltpu.VMEM((chunks, BIN_DEV, WIDTH), f32),
+            pltpu.VMEM((chunks, BIN_DEV, WIDTH), bf16),
+            pltpu.VMEM((chunks, BIN_DEV, WIDTH), bf16),
+            pltpu.VMEM((chunks - 2, BIN_DEV, WIDTH), bf16),
+            pltpu.VMEM((chunks - 2, BIN_DEV, WIDTH), bf16),
+            pltpu.VMEM((8, 2 * BIN_DEV), f32),
+            pltpu.VMEM((8, 2 * BIN_DEV), f32),
+            pltpu.VMEM((2, 8, BIN_DEV), f32),
+            pltpu.VMEM((8, BIN_DEV), f32),
+            pltpu.VMEM((3, 8, BIN_DEV), f32),
+            dma,
+            dma((chunks,)),
+            dma((chunks,)),
+            dma((chunks,)),
+            dma((chunks,)),
+            dma((chunks,)),
+            dma((chunks - 2,)),
+            dma((chunks - 2,)),
+            dma((5,)),
+            dma((5,)),
+        ],
+        compiler_params=pltpu.CompilerParams(
+            collective_id=0, has_side_effects=True, vmem_limit_bytes=48 * 2**20
+        ),
+        cost_estimate=pl.CostEstimate(
+            flops=4 * rows * samples * span, bytes_accessed=4 * rows * samples, transcendentals=0
+        ),
+    )(
+        shot_traces[0],
+        nmo_weight[0],
+        trace_owner.reshape(1, rows),
+        trace_bin,
+        band_start[0],
+        mute_start,
+    )
+    return totals / jnp.maximum(fold[0], 1.0)[:, None]
+
+
 def solution(mesh):
+    direct = mesh.shape["cmp"] == 4 and mesh.shape["off"] == 4
     return jax.shard_map(
-        on_device,
+        on_device_fused if direct else on_device,
         mesh=mesh,
         in_specs=(
             P(("groups", "off"), "cmp", None),

time: 163 us -> 32.9 us (0.20)
  matrix products: 49.3 us -> 0 us
  between operations: 44 us -> 0.68 us
  waiting for transfers between devices: 30.9 us -> 0 us
  Pallas kernels: 0 us -> 26 us
  blocking collectives: 13.1 us -> 0 us
  starting transfers between devices: 8.54 us -> 0 us
  local copies, waits for them, and re-layouts: 10.3 us -> 5.19 us
  other arithmetic: 5.59 us -> 0.8 us
    dot_general x17 -> x0, matrix products: 49.3 us -> none  [the longest x16 43.2 us: correct_traces(): jnp.dot(source, weight[window], preferred_element_type=jnp.float32)]
    pallas_call x0 -> x1, Pallas kernels: none -> 26 us  [on_device_fused(): pl.pallas_call(fused, out_shape=(jax.ShapeDtypeStruct((BIN_DEV, samples /...]
    reduce_scatter x1 -> x0, waiting for transfers between devices: 16.6 us -> none  [on_device(): lax.psum_scatter(partial_stack, 'off', scatter_dimension=1, tiled=True)]
    all_to_all x2 -> x0, waiting for transfers between devices: 14.2 us -> none  [the longest x1 14.2 us: on_device(): lax.all_to_all(buffer.reshape(peer_count, capacity, samples), 'cmp', spli...]
    psum x1 -> x0, blocking collectives: 13.1 us -> none  [on_device(): fold_count = lax.psum(local_fold, 'off')]
    scatter x2 -> x0, local copies, waits for them, and re-layouts: 9.34 us -> none  [the longest x1 6.17 us: on_device(): jnp.zeros((peer_count * capacity, samples), jnp.bfloat16).at[target]]
    all_to_all x2 -> x0, starting transfers between devices: 8.31 us -> none  [the longest x1 5.07 us: on_device(): lax.all_to_all(buffer.reshape(peer_count, capacity, samples), 'cmp', spli...]
    unnamed x6 -> x10, local copies, waits for them, and re-layouts: 0.01 us -> 5.19 us
  transfers between devices with their start and end apart: 3 -> 0, of which waited for: 2 -> 0; matrix products, arithmetic and copies ran while one was open for 29% -> 0% of each run, Pallas kernels for 0% -> 0%
where the time goes in v1:
time: 32.9 us; the launch traced here: 32.6 us
  Pallas kernels  26 us (79%)
  local copies, waits for them, and re-layouts  5.19 us (16%)
  other arithmetic  0.8 us (2%)
  between operations  0.68 us (2%)
    pallas_call x1, Pallas kernels, on_device_fused(): pl.pallas_call(fused, out_shape=(jax.ShapeDtypeStruct((BIN_DEV, samples /...  26 us
    unnamed x10, local copies, waits for them, and re-layouts  5.19 us
    div x1, other arithmetic, on_device_fused(): return totals / jnp.maximum(fold[0], 1.0)[:, None]  0.8 us

profile of v1, /device:TPU:0, one launch (start us, length us, event | category | flops | bytes accessed | tf_op | source)
XLA Modules:
  0.0 32.6 jit_solution(9142681986524880930)
XLA Ops:
  0.7 0.0 copy-start
  0.7 1.6 %copy-done = bf16[1,512,2048]{2,1,0:T(8,128)(2,1)S(1)} copy-done((bf16[1,512,2048]{2,1,0:T(8,128)(2,1)S(1)}, bf16[1,512,2048]{2,1,0:T(8,128)(2,1)}, u32[]{:S(2)}) %copy-start) | copy-done | bytes 2097176
  2.2 0.0 copy-start.1
  2.2 1.6 %copy-done.1 = bf16[1,16,512,128]{3,2,1,0:T(8,128)(2,1)S(1)} copy-done((bf16[1,16,512,128]{3,2,1,0:T(8,128)(2,1)S(1)}, bf16[1,16,512,128]{3,2,1,0:T(8,128)(2,1)}, u32[]{:S(2)}) %copy-start.1) | copy-done | bytes 2097176
  3.8 0.0 copy-start.2
  3.8 0.7 %copy-done.2 = s32[1,512,1]{1,2,0:T(1,128)S(1)} copy-done((s32[1,512,1]{1,2,0:T(1,128)S(1)}, s32[1,512,1]{1,2,0:T(1,128)}, u32[]{:S(2)}) %copy-start.2) | copy-done | bytes 2072
  4.5 0.0 copy-start.3
  4.5 0.7 %copy-done.3 = s32[1,512]{1,0:T(1,128)S(1)} copy-done((s32[1,512]{1,0:T(1,128)S(1)}, s32[1,512]{1,0:T(1,128)}, u32[]{:S(2)}) %copy-start.3) | copy-done | bytes 2072
  5.2 0.0 copy-start.4
  5.2 0.7 %copy-done.4 = s32[1,16]{1,0:T(1,128)S(1)} copy-done((s32[1,16]{1,0:T(1,128)S(1)}, s32[1,16]{1,0:T(1,128)}, u32[]{:S(2)}) %copy-start.4) | copy-done | bytes 88
  5.9 26.0 %shard_map.64 = (f32[128,512]{1,0:T(8,128)S(1)}, f32[8,128]{1,0:T(8,128)S(1)}) custom-call(bf16[512,2048]{1,0:T(8,128)(2,1)S(1)} %bitcast.6, bf16[16,512,128]{2,1,0:T(8,128)(2,1)S(1)} %bitcast.7, s32[1,512]{1,0:T(1,128)S(1)} %bitcast.8, s32[1,512]{1,0:T(1,128)S(1)} %copy-done.3, s32[16]{0:T(128)S(1)} %bitcast.9, f32[1]{0:T(128)S(6)} %copy.7.mute_ref), custom_call_target="tpu_custom_call" | custom-call | flops 2147483648 | bytes 4194304 | tf_op jit(solution)/shard_map/pallas_call | solution.py:276
  31.8 0.8 %broadcast_divide_fusion = f32[128,512]{1,0:T(8,128)} fusion(f32[128,512]{1,0:T(8,128)S(1)} %get-tuple-element.7, f32[128]{0:T(128)S(1)} %maximum_bitcast_fusion), kind=kLoop, calls=%fused_computation | loop fusion | flops 65536 | bytes 524800 | tf_op jit(solution)/shard_map/div | solution.py:328
  (1 shorter events, 0.0 us)
Async XLA Ops:
  0.7 1.6 %copy-start = (bf16[1,512,2048]{2,1,0:T(8,128)(2,1)S(1)}, bf16[1,512,2048]{2,1,0:T(8,128)(2,1)}, u32[]{:S(2)}) copy-start(bf16[1,512,2048]{2,1,0:T(8,128)(2,1)} %param.6) | copy-start | bytes 6291460
  2.2 1.6 %copy-start.1 = (bf16[1,16,512,128]{3,2,1,0:T(8,128)(2,1)S(1)}, bf16[1,16,512,128]{3,2,1,0:T(8,128)(2,1)}, u32[]{:S(2)}) copy-start(bf16[1,16,512,128]{3,2,1,0:T(8,128)(2,1)} %param.9) | copy-start | bytes 6291460
  3.8 0.7 %copy-start.2 = (s32[1,512,1]{1,2,0:T(1,128)S(1)}, s32[1,512,1]{1,2,0:T(1,128)}, u32[]{:S(2)}) copy-start(s32[1,512,1]{1,2,0:T(1,128)} %param.7) | copy-start | bytes 6148
  4.5 0.7 %copy-start.3 = (s32[1,512]{1,0:T(1,128)S(1)}, s32[1,512]{1,0:T(1,128)}, u32[]{:S(2)}) copy-start(s32[1,512]{1,0:T(1,128)} %bin_ref.1) | copy-start | bytes 6148
  5.2 0.7 %copy-start.4 = (s32[1,16]{1,0:T(1,128)S(1)}, s32[1,16]{1,0:T(1,128)}, u32[]{:S(2)}) copy-start(s32[1,16]{1,0:T(1,128)} %param.10) | copy-start | bytes 196

commit v2 on v1

--- a/solution.py
+++ b/solution.py
@@ -71,13 +71,14 @@
 
 
 def fused(
-    traces_hbm, weight_hbm, owner_ref, bin_ref, starts_ref, mute_ref,
+    traces_hbm, weight_hbm, owner_hbm, bin_hbm, starts_hbm, mute_hbm,
     out_ref, fold_ref,
+    owner_ref, bin_ref, starts_ref, mute_ref,
     traces, weight, padded, shifted_weight, selector,
     keep_core, send_core, recv_core,
     keep_x, send_x, recv_x, send_z, recv_z,
     fold_core_out, fold_core_in, fold_x_out, fold_x_in, fold_z_in,
-    load_sem, weight_sem,
+    load_sem, small_sem, weight_sem,
     core_send_sem, core_recv_sem, x_send_sem, x_recv_sem, z_send_sem, z_recv_sem,
     fold_send_sem, fold_recv_sem,
 ):
@@ -102,6 +103,19 @@
     def pair_of(m):
         return 2 * lax.rem(z + 1 + m // 2, nz) + m % 2
 
+    small = [
+        pltpu.make_async_copy(source, target, small_sem.at[slot])
+        for slot, (source, target) in enumerate(
+            (
+                (owner_hbm, owner_ref),
+                (bin_hbm, bin_ref),
+                (starts_hbm, starts_ref),
+                (mute_hbm, mute_ref),
+            )
+        )
+    ]
+    for copy in small:
+        copy.start()
     load = pltpu.make_async_copy(traces_hbm, traces, load_sem)
     load.start()
 
@@ -116,6 +130,8 @@
 
     lax.fori_loop(0, chunks, begin, 0)
 
+    for copy in small:
+        copy.wait()
     owner = owner_ref[...]
     other_core = jnp.where(lax.rem(owner, 2) == lax.rem(c, 2), 0, 1)
     other_x = jnp.where(owner // 2 == c // 2, 0, 1)
@@ -269,9 +285,8 @@
     windows, span, ws = nmo_weight.shape[1:]
     chunks = samples // WIDTH
     f32, bf16 = jnp.float32, jnp.bfloat16
-    any_space = pl.BlockSpec(memory_space=pl.ANY)
+    hbm = pl.BlockSpec(memory_space=pltpu.HBM)
     vmem = pl.BlockSpec(memory_space=pltpu.VMEM)
-    smem = pl.BlockSpec(memory_space=pltpu.SMEM)
     dma = pltpu.SemaphoreType.DMA
     totals, fold = pl.pallas_call(
         fused,
@@ -279,9 +294,13 @@
             jax.ShapeDtypeStruct((BIN_DEV, samples // 4), f32),
             jax.ShapeDtypeStruct((8, BIN_DEV), f32),
         ),
-        in_specs=[any_space, any_space, vmem, vmem, smem, smem],
+        in_specs=[hbm] * 6,
         out_specs=(vmem, vmem),
         scratch_shapes=[
+            pltpu.VMEM((1, rows), jnp.int32),
+            pltpu.VMEM((1, rows), jnp.int32),
+            pltpu.SMEM((windows,), jnp.int32),
+            pltpu.SMEM((1,), f32),
             pltpu.VMEM((rows, samples), bf16),
             pltpu.VMEM((chunks, 2, span, ws), bf16),
             pltpu.VMEM((2, span + 2 * SPREAD, ws), f32),
@@ -301,6 +320,7 @@
             pltpu.VMEM((8, BIN_DEV), f32),
             pltpu.VMEM((3, 8, BIN_DEV), f32),
             dma,
+            dma((4,)),
             dma((chunks,)),
             dma((chunks,)),
             dma((chunks,)),
@@ -312,7 +332,7 @@
             dma((5,)),
         ],
         compiler_params=pltpu.CompilerParams(
-            collective_id=0, has_side_effects=True, vmem_limit_bytes=48 * 2**20
+            collective_id=0, has_side_effects=True, vmem_limit_bytes=62 * 2**20
         ),
         cost_estimate=pl.CostEstimate(
             flops=4 * rows * samples * span, bytes_accessed=4 * rows * samples, transcendentals=0

time: 32.9 us -> 30.4 us (0.924)
  local copies, waits for them, and re-layouts: 5.19 us -> 0 us
  other arithmetic: 0.8 us -> 2.43 us
  Pallas kernels: 26 us -> 27.1 us
    unnamed x10 -> x0, local copies, waits for them, and re-layouts: 5.19 us -> none
    pallas_call x1, Pallas kernels: 26 us -> 27.1 us  [on_device_fused(): pl.pallas_call(fused, out_shape=(jax.ShapeDtypeStruct((BIN_DEV, samples /...]
    div x1, other arithmetic: 0.8 us -> 1.74 us  [on_device_fused(): return totals / jnp.maximum(fold[0], 1.0)[:, None]]
    max x1, other arithmetic: 0.01 us -> 0.69 us  [on_device_fused(): return totals / jnp.maximum(fold[0], 1.0)[:, None]]
where the time goes in v2:
time: 30.4 us; the launch traced here: 30.2 us
  Pallas kernels  27.1 us (89%)
  other arithmetic  2.43 us (8%)
  between operations  0.66 us (2%)
    pallas_call x1, Pallas kernels, on_device_fused(): pl.pallas_call(fused, out_shape=(jax.ShapeDtypeStruct((BIN_DEV, samples /...  27.1 us
    div x1, other arithmetic, on_device_fused(): return totals / jnp.maximum(fold[0], 1.0)[:, None]  1.74 us
    max x1, other arithmetic, on_device_fused(): return totals / jnp.maximum(fold[0], 1.0)[:, None]  0.69 us

profile of v2, /device:TPU:0, one launch (start us, length us, event | category | flops | bytes accessed | tf_op | source)
XLA Modules:
  0.0 30.2 jit_solution(10125269438176653750)
XLA Ops:
  0.7 27.1 %shard_map.64 = (f32[128,512]{1,0:T(8,128)}, f32[8,128]{1,0:T(8,128)}) custom-call(bf16[512,2048]{1,0:T(8,128)(2,1)} %bitcast.6, bf16[16,512,128]{2,1,0:T(8,128)(2,1)} %bitcast.7, s32[1,512]{1,0:T(1,128)} %bitcast.8, s32[1,512]{1,0:T(1,128)} %bin_hbm.1, s32[16]{0:T(128)} %bitcast.9, f32[1]{0:T(128)S(6)} %copy.7.mute_hbm), custom_call_target="tpu_custom_call" | custom-call | flops 2147483648 | bytes 4194304 | tf_op jit(solution)/shard_map/pallas_call | solution.py:291
  27.7 0.7 %maximum_bitcast_fusion = f32[128]{0:T(128)S(1)} fusion(f32[8,128]{1,0:T(8,128)} %get-tuple-element.8), kind=kLoop, calls=%fused_computation.1 | loop fusion | flops 128 | bytes 1024 | tf_op jit(solution)/shard_map/max | solution.py:348
  28.4 1.7 %broadcast_divide_fusion = f32[128,512]{1,0:T(8,128)} fusion(f32[128,512]{1,0:T(8,128)} %get-tuple-element.7, f32[128]{0:T(128)S(1)} %maximum_bitcast_fusion), kind=kLoop, calls=%fused_computation | loop fusion | flops 65536 | bytes 524800 | tf_op jit(solution)/shard_map/div | solution.py:348

commit v3 on v2

--- a/solution.py
+++ b/solution.py
@@ -74,11 +74,11 @@
     traces_hbm, weight_hbm, owner_hbm, bin_hbm, starts_hbm, mute_hbm,
     out_ref, fold_ref,
     owner_ref, bin_ref, starts_ref, mute_ref,
-    traces, weight, padded, shifted_weight, selector,
+    traces, first_band, weight, padded, shifted_weight, selector,
     keep_core, send_core, recv_core,
     keep_x, send_x, recv_x, send_z, recv_z,
     fold_core_out, fold_core_in, fold_x_out, fold_x_in, fold_z_in,
-    load_sem, small_sem, weight_sem,
+    load_sem, first_sem, small_sem, weight_sem,
     core_send_sem, core_recv_sem, x_send_sem, x_recv_sem, z_send_sem, z_recv_sem,
     fold_send_sem, fold_recv_sem,
 ):
@@ -101,7 +101,7 @@
         )
 
     def pair_of(m):
-        return 2 * lax.rem(z + 1 + m // 2, nz) + m % 2
+        return 2 * lax.rem(z + nz - 1 - m // 2, nz) + m % 2
 
     small = [
         pltpu.make_async_copy(source, target, small_sem.at[slot])
@@ -116,8 +116,16 @@
     ]
     for copy in small:
         copy.start()
+    def base_of(m):
+        pair = pair_of(m)
+        last = samples - band
+        return WIDTH * pair - (pair // -(-last // WIDTH)) * (WIDTH * pair - last)
+
+    first_load = pltpu.make_async_copy(
+        traces_hbm.at[:, pl.ds(pl.multiple_of(base_of(0), 128), band)], first_band, first_sem
+    )
+    first_load.start()
     load = pltpu.make_async_copy(traces_hbm, traces, load_sem)
-    load.start()
 
     def weight_load(m):
         return pltpu.make_async_copy(
@@ -128,7 +136,7 @@
         weight_load(m).start()
         return carry
 
-    lax.fori_loop(0, chunks, begin, 0)
+    weight_load(0).start()
 
     for copy in small:
         copy.wait()
@@ -147,7 +155,10 @@
     fold_core_out[...] = fold[:, 2 * BIN_DEV :]
     padded[:, 0:SPREAD] = jnp.zeros((2, SPREAD, 128), jnp.float32)
     padded[:, SPREAD + span :] = jnp.zeros((2, SPREAD, 128), jnp.float32)
-    load.wait()
+    first_load.wait()
+    weight_load(0).wait()
+    load.start()
+    lax.fori_loop(1, chunks, begin, 0)
 
     def core_copy(m):
         return pltpu.make_async_remote_copy(
@@ -167,7 +178,7 @@
         return pltpu.make_async_remote_copy(
             src_ref=send_z.at[m], dst_ref=recv_z.at[m],
             send_sem=z_send_sem.at[m], recv_sem=z_recv_sem.at[m],
-            device_id={"off": lax.rem(z + 1 + m // 2, nz)}, device_id_type=MESH,
+            device_id={"off": lax.rem(z + nz - 1 - m // 2, nz)}, device_id_type=MESH,
         )
 
     def fold_copy(source, target, slot, device):
@@ -177,10 +188,9 @@
             device_id=device, device_id_type=MESH,
         )
 
-    def correct(m):
-        weight_load(m).wait()
+    def correct(m, source):
         first = pair_of(m) * WIDTH
-        base = jnp.minimum(first, samples - band)
+        base = base_of(m)
         for half in range(2):
             start = starts_ref[2 * pair_of(m) + half]
             lead = jnp.clip(start - base, 0, SPREAD)
@@ -188,8 +198,7 @@
             shifted_weight[:, half * 128 : half * 128 + 128] = padded[
                 half, pl.ds(SPREAD - lead, band)
             ].astype(jnp.bfloat16)
-        source = traces[:, pl.ds(pl.multiple_of(base, 128), band)]
-        shifted = jnp.dot(source, shifted_weight[...], preferred_element_type=jnp.float32)
+        shifted = jnp.dot(source(), shifted_weight[...], preferred_element_type=jnp.float32)
         time = first + lax.broadcasted_iota(jnp.int32, (1, WIDTH), 1)
         taper = jnp.clip((time.astype(jnp.float32) - mute_ref[0]) / ramp_width, 0.0, 1.0)
         corrected = (shifted * taper).astype(jnp.bfloat16)
@@ -212,16 +221,28 @@
         send_z[m] = x_total(m).astype(jnp.bfloat16)
         z_copy(m).start()
 
-    correct(0)
+    def later(m):
+        weight_load(m).wait()
+        correct(m, lambda: traces[:, pl.ds(pl.multiple_of(base_of(m), 128), band)])
+        core_copy(m).start()
+        end_core(m - 1)
+
+    correct(0, lambda: first_band[...])
     pl.semaphore_wait(barrier, nz + 1)
     core_copy(0).start()
     fold_core = fold_copy(fold_core_out, fold_core_in, 0, {"cmp": core_peer})
     fold_core.start()
+    load.wait()
+    later(1)
+    fold_core.wait_recv()
+    fold = fold[:, : 2 * BIN_DEV] + fold_core_in[...]
+    fold_x_out[0] = fold[:, BIN_DEV:]
+    fold_x_out[1] = fold[:, :BIN_DEV]
+    fold_x = fold_copy(fold_x_out.at[0], fold_x_in, 1, {"cmp": x_peer})
+    fold_x.start()
 
     def step(m, carry):
-        correct(m)
-        core_copy(m).start()
-        end_core(m - 1)
+        later(m)
 
         @pl.when(m >= 3)
         def _():
@@ -229,55 +250,60 @@
 
         return carry
 
-    lax.fori_loop(1, chunks, step, 0)
+    lax.fori_loop(2, chunks, step, 0)
     end_core(chunks - 1)
 
-    fold_core.wait_recv()
-    fold = fold[:, : 2 * BIN_DEV] + fold_core_in[...]
-    fold_x_out[0] = fold[:, BIN_DEV:]
-    fold_x = fold_copy(fold_x_out.at[0], fold_x_in, 1, {"cmp": x_peer})
-    fold_x.start()
-    for m in range(chunks - 3, chunks - 2):
-        end_x(m)
     fold_x.wait_recv()
-    fold = fold[:, :BIN_DEV] + fold_x_in[...]
-    fold_x_out[1] = fold
+    fold = fold_x_out[1] + fold_x_in[...]
+    fold_x_out[2] = fold
     fold_z = []
     for away in range(1, nz):
         copy = fold_copy(
-            fold_x_out.at[1], fold_z_in.at[away - 1], 1 + away, {"off": lax.rem(z + away, nz)}
+            fold_x_out.at[2], fold_z_in.at[away - 1], 1 + away, {"off": lax.rem(z + away, nz)}
         )
         copy.start()
         fold_z.append(copy)
-
-    for half in range(2):
-        out_ref[:, half * WIDTH : half * WIDTH + WIDTH] = x_total(chunks - 2 + half)
+    for m in range(chunks - 3, chunks - 2):
+        end_x(m)
+
+    def drain(m, carry):
+        core_copy(m).wait_send()
+        return carry
+
+    lax.fori_loop(0, chunks, drain, 0)
+    fold_core.wait_send()
+    fold_x.wait_send()
     for copy in fold_z:
         copy.wait_recv()
     for away in range(1, nz):
         fold = fold + fold_z_in[away - 1]
     fold_ref[...] = fold
-    for m in range(chunks - 2):
-        z_copy(m).wait_recv()
-        half = m % 2
-        out_ref[:, half * WIDTH : half * WIDTH + WIDTH] += recv_z[m].astype(jnp.float32)
-
-    def drain(m, carry):
-        core_copy(m).wait_send()
+    for copy in fold_z:
+        copy.wait_send()
+
+    def drain_x(m, carry):
         x_copy(m).wait_send()
         return carry
 
-    lax.fori_loop(0, chunks, drain, 0)
-
-    def drain_z(m, carry):
+    lax.fori_loop(0, chunks - 2, drain_x, 0)
+    early = [None, None]
+    for m in range(chunks - 4):
+        z_copy(m).wait_recv()
         z_copy(m).wait_send()
-        return carry
-
-    lax.fori_loop(0, chunks - 2, drain_z, 0)
-    fold_core.wait_send()
-    fold_x.wait_send()
-    for copy in fold_z:
-        copy.wait_send()
+        arrived = recv_z[m].astype(jnp.float32)
+        early[m % 2] = arrived if m < 2 else early[m % 2] + arrived
+    for half in range(2):
+        out_ref[:, half * WIDTH : half * WIDTH + WIDTH] = early[half]
+    for m in range(chunks - 2, chunks):
+        half = m % 2
+        out_ref[:, half * WIDTH : half * WIDTH + WIDTH] += x_total(m)
+    for m in range(chunks - 4, chunks - 2):
+        half = m % 2
+        z_copy(m).wait_recv()
+        out_ref[:, half * WIDTH : half * WIDTH + WIDTH] += recv_z[m].astype(jnp.float32)
+        z_copy(m).wait_send()
+    for m in range(chunks - 2, chunks):
+        x_copy(m).wait_send()
 
 
 def on_device_fused(shot_traces, trace_owner, trace_bin, nmo_weight, band_start, mute_start):
@@ -302,6 +328,7 @@
             pltpu.SMEM((windows,), jnp.int32),
             pltpu.SMEM((1,), f32),
             pltpu.VMEM((rows, samples), bf16),
+            pltpu.VMEM((rows, span + SPREAD), bf16),
             pltpu.VMEM((chunks, 2, span, ws), bf16),
             pltpu.VMEM((2, span + 2 * SPREAD, ws), f32),
             pltpu.VMEM((span + SPREAD, WIDTH), bf16),
@@ -316,9 +343,10 @@
             pltpu.VMEM((chunks - 2, BIN_DEV, WIDTH), bf16),
             pltpu.VMEM((8, 2 * BIN_DEV), f32),
             pltpu.VMEM((8, 2 * BIN_DEV), f32),
-            pltpu.VMEM((2, 8, BIN_DEV), f32),
+            pltpu.VMEM((3, 8, BIN_DEV), f32),
             pltpu.VMEM((8, BIN_DEV), f32),
             pltpu.VMEM((3, 8, BIN_DEV), f32),
+            dma,
             dma,
             dma((4,)),
             dma((chunks,)),
@@ -332,17 +360,22 @@
             dma((5,)),
         ],
         compiler_params=pltpu.CompilerParams(
-            collective_id=0, has_side_effects=True, vmem_limit_bytes=62 * 2**20
+            collective_id=0, has_side_effects=True, vmem_limit_bytes=48 * 2**20
         ),
         cost_estimate=pl.CostEstimate(
             flops=4 * rows * samples * span, bytes_accessed=4 * rows * samples, transcendentals=0
         ),
     )(
-        shot_traces[0],
-        nmo_weight[0],
-        trace_owner.reshape(1, rows),
-        trace_bin,
-        band_start[0],
+        *(
+            pltpu.with_memory_space_constraint(array, pltpu.HBM)
+            for array in (
+                shot_traces[0],
+                nmo_weight[0],
+                trace_owner.reshape(1, rows),
+                trace_bin,
+                band_start[0],
+            )
+        ),
         mute_start,
     )
     return totals / jnp.maximum(fold[0], 1.0)[:, None]

time: 30.4 us -> 27 us (0.89)
  Pallas kernels: 27.1 us -> 25.3 us
  other arithmetic: 2.43 us -> 0.8 us
    pallas_call x1, Pallas kernels: 27.1 us -> 25.3 us  [on_device_fused(): pl.pallas_call(fused, out_shape=(jax.ShapeDtypeStruct((BIN_DEV, samples /...]
    div x1, other arithmetic: 1.74 us -> 0.8 us  [on_device_fused(): return totals / jnp.maximum(fold[0], 1.0)[:, None]]
    max x1, other arithmetic: 0.69 us -> 0.01 us  [on_device_fused(): return totals / jnp.maximum(fold[0], 1.0)[:, None]]
where the time goes in v3:
time: 27 us; the launch traced here: 26.8 us
  Pallas kernels  25.3 us (94%)
  other arithmetic  0.8 us (3%)
  between operations  0.67 us (2%)
    pallas_call x1, Pallas kernels, on_device_fused(): pl.pallas_call(fused, out_shape=(jax.ShapeDtypeStruct((BIN_DEV, samples /...  25.3 us
    div x1, other arithmetic, on_device_fused(): return totals / jnp.maximum(fold[0], 1.0)[:, None]  0.8 us

profile of v3, /device:TPU:0, one launch (start us, length us, event | category | flops | bytes accessed | tf_op | source)
XLA Modules:
  0.0 26.8 jit_solution(17977294620609603871)
XLA Ops:
  0.7 25.3 %shard_map.64 = (f32[128,512]{1,0:T(8,128)S(1)}, f32[8,128]{1,0:T(8,128)S(1)}) custom-call(bf16[512,2048]{1,0:T(8,128)(2,1)} %bitcast.6, bf16[16,512,128]{2,1,0:T(8,128)(2,1)} %bitcast.7, s32[1,512]{1,0:T(1,128)} %bitcast.8, s32[1,512]{1,0:T(1,128)} %bin_hbm.1, s32[16]{0:T(128)} %bitcast.9, f32[1]{0:T(128)S(6)} %copy.7.mute_hbm), custom_call_target="tpu_custom_call" | custom-call | flops 2147483648 | bytes 4194304 | tf_op jit(solution)/shard_map/pallas_call | solution.py:317
  26.0 0.8 %broadcast_divide_fusion = f32[128,512]{1,0:T(8,128)} fusion(f32[128,512]{1,0:T(8,128)S(1)} %get-tuple-element.7, f32[128]{0:T(128)S(1)} %maximum_bitcast_fusion), kind=kLoop, calls=%fused_computation | loop fusion | flops 65536 | bytes 524800 | tf_op jit(solution)/shard_map/div | solution.py:381
  (1 shorter events, 0.0 us)
